TPU v7x, 256 devices: a whole 4x4x8 slice. The times are simulated.
256 devices in a mesh: segment: 4 (over z_hi), mp: 16 (over y, x), dp: 4 (over z_lo, core).
Axes of the slice: x: 4, y: 4, z: 8 (z_hi: 4, z_lo: 2; z = z_hi * 2 + z_lo), core: 2. Of those that a mesh axis runs over, the one named last changes fastest.
Arguments:
- frames: bfloat16 [128, 128, 1536], P(('segment', 'dp'), 'mp'), may hold values from -6 to 6
- latent_init: bfloat16 [64, 1536], replicated, may hold values from -6 to 6
- norm_gains: bfloat16 [3, 1536], replicated, may hold values from 0.099609375 to 1.8984375
- res_query: bfloat16 [1536, 1536], P(None, 'mp'), may hold values from -0.15625 to 0.15625
- res_kv: bfloat16 [1536, 2, 1536], P(None, None, 'mp'), may hold values from -0.15625 to 0.15625
- res_out: bfloat16 [1536, 1536], replicated, may hold values from -0.15625 to 0.15625
- text: bfloat16 [4, 4, 768, 8192], P('segment', 'dp', None, 'mp'), may hold values from -6 to 6
- text_gain: bfloat16 [4, 8192], P('segment'), may hold values from 0.099609375 to 1.8984375
- w_query: bfloat16 [4, 8192, 8192], P('segment', 'dp', 'mp'), may hold values from -0.0625 to 0.0625
- w_kv: bfloat16 [4, 1536, 2, 8192], P('segment', 'dp', None, 'mp'), may hold values from -0.15625 to 0.15625
- xgate: float32 [4], P('segment'), may hold values from 0.3 to 1.2
- frame_counts: int32 [4, 4], P('segment', 'dp'), may hold values from 1 to 8
- frame_dest: int32 [128], replicated, may hold values from 0 to 127, each once
- cotangent: bfloat16 [4, 4, 768, 8192], P('segment', 'dp', None, 'mp'), may hold values from -6 to 6
Outputs:
- context: bfloat16 [4, 4, 768, 8192], P('segment', 'dp', None, 'mp')
- latent_grad: float32 [64, 128, 1536], P('mp', ('segment', 'dp'))
Inputs may be any that keep to these rules, and one draw needn't show every extreme that they name: frame_dest is a permutation of the slots; a slot is used by its destination sequence only if its frame number is below that sequence's frame count.
All inputs are finite; a program needn't handle non-finite values.
Results may differ from a plain program's by a relative error of at most 0.04.
Values may be sent and summed in bfloat16 or wider, within the bound.
No kernel may reach another device: no remote copies, remote signals or barrier semaphores. Data moves between devices by JAX's collectives and lax.ppermute only.
A program may use at most 128 MiB of HBM per device.

v0:
```python
import math
import jax
import jax.numpy as jnp
from jax import lax
from jax.sharding import PartitionSpec as P

HD = 128
E = 1536
RESAMPLE_HEAD_DIM = 96
LAT = 64
FMAX = 8


def layer_norm(inputs, gain_row):
    values = inputs.astype(jnp.float32)
    center = values - jnp.mean(values, axis=-1, keepdims=True)
    spread = jnp.mean(center * center, axis=-1, keepdims=True)
    return center * lax.rsqrt(spread + 1e-05) * gain_row.astype(jnp.float32)


def attend(query_matrix, key_value_block, live, gate):
    score_matrix = jnp.einsum(
        "rag,lag->arl", query_matrix, key_value_block[:, 0], preferred_element_type=jnp.float32
    ) / math.sqrt(query_matrix.shape[-1])
    score_matrix = jnp.where(live[None, None, :], score_matrix, -1e30)
    row_max = lax.stop_gradient(jnp.max(score_matrix, axis=-1, keepdims=True))
    unnormalized_weights = jnp.exp(score_matrix - row_max)
    row_sum = jnp.sum(unnormalized_weights, axis=-1)
    blended_values = jnp.einsum(
        "lfv,vla->fla",
        unnormalized_weights.astype(jnp.bfloat16),
        key_value_block[:, 1],
        preferred_element_type=jnp.float32,
    )
    blended_values = blended_values / jnp.transpose(row_sum)[:, :, None]
    return gate * blended_values.reshape(blended_values.shape[0], -1)


def per_device(
    frames,
    latent_init,
    norm_gains,
    res_query,
    res_kv,
    res_out,
    text,
    text_gain,
    w_query,
    w_kv,
    xgate,
    frame_counts,
    frame_dest,
    cotangent,
):
    mp_count = lax.axis_size("mp")
    share = LAT // mp_count
    slots = frame_dest.shape[0]
    owned = frames.shape[0]
    res_cols = res_query.shape[1]
    res_local = res_cols // RESAMPLE_HEAD_DIM
    res_scale = 1.0 / math.sqrt(RESAMPLE_HEAD_DIM)
    lat_norm = layer_norm(latent_init, norm_gains[1]).astype(jnp.bfloat16)
    resampler_heads = (
        jnp.dot(lat_norm, res_query, preferred_element_type=jnp.float32)
        .astype(jnp.bfloat16)
        .reshape(LAT, res_local, RESAMPLE_HEAD_DIM)
    )
    latent_pair_rows = (
        jnp.einsum("le,ekc->lkc", lat_norm, res_kv, preferred_element_type=jnp.float32)
        .astype(jnp.bfloat16)
        .reshape(LAT, 2, res_local, RESAMPLE_HEAD_DIM)
    )
    first_scores = (
        jnp.einsum(
            "epg,apg->pea",
            resampler_heads,
            latent_pair_rows[:, 0],
            preferred_element_type=jnp.float32,
        )
        * res_scale
    )
    first_max = jnp.max(first_scores, axis=-1)
    first_exp = jnp.exp(first_scores - first_max[:, :, None])
    first_sum = jnp.sum(first_exp, axis=-1)
    first_acc = jnp.einsum(
        "nvf,fnr->nvr",
        first_exp.astype(jnp.bfloat16),
        latent_pair_rows[:, 1],
        preferred_element_type=jnp.float32,
    )
    piece = lax.all_gather(frames, "mp", axis=1, tiled=True)
    run_max = jnp.broadcast_to(first_max, (owned,) + first_max.shape)
    run_sum = jnp.broadcast_to(first_sum, (owned,) + first_sum.shape)
    run_acc = jnp.broadcast_to(first_acc, (owned,) + first_acc.shape)
    width = piece.shape[1]
    media = layer_norm(piece, norm_gains[0]).astype(jnp.bfloat16)
    media_pairs = (
        jnp.einsum("fpe,ekc->fpkc", media, res_kv, preferred_element_type=jnp.float32)
        .astype(jnp.bfloat16)
        .reshape(owned, width, 2, res_local, RESAMPLE_HEAD_DIM)
    )
    score_matrix = (
        jnp.einsum(
            "lhd,fphd->fhlp",
            resampler_heads,
            media_pairs[:, :, 0],
            preferred_element_type=jnp.float32,
        )
        * res_scale
    )
    new_max = jnp.maximum(run_max, jnp.max(score_matrix, axis=-1))
    fade = jnp.exp(run_max - new_max)
    unnormalized_weights = jnp.exp(score_matrix - new_max[..., None])
    new_sum = run_sum * fade + jnp.sum(unnormalized_weights, axis=-1)
    new_acc = run_acc * fade[..., None] + jnp.einsum(
        "fhlp,fphd->fhld",
        unnormalized_weights.astype(jnp.bfloat16),
        media_pairs[:, :, 1],
        preferred_element_type=jnp.float32,
    )
    res_context = (new_acc / new_sum[..., None]).astype(jnp.bfloat16)
    out_rows = lax.dynamic_slice_in_dim(res_out, lax.axis_index("mp") * res_cols, res_cols, 0)
    out_heads = out_rows.reshape(res_local, RESAMPLE_HEAD_DIM, E)
    part = res_context
    update = lax.psum_scatter(
        jnp.einsum("fhlr,hre->lfe", part, out_heads, preferred_element_type=jnp.float32).astype(
            jnp.bfloat16
        ),
        "mp",
        scatter_dimension=0,
        tiled=True,
    ).astype(jnp.float32)
    base_rows = lax.dynamic_slice_in_dim(
        latent_init, lax.axis_index("mp") * share, share, 0
    ).astype(jnp.float32)
    latents = layer_norm(base_rows[:, None, :] + update, norm_gains[2]).astype(jnp.bfloat16)
    gathered = lax.all_gather(latents, ("segment", "dp"), axis=1, tiled=True)
    group = lax.axis_index(("segment", "dp"))
    wanted = group * owned + jnp.arange(owned, dtype=jnp.int32)
    picker = (frame_dest[None, :] == wanted[:, None]).astype(jnp.bfloat16)
    mine = jnp.einsum("js,rse->rje", picker, gathered, preferred_element_type=jnp.float32).astype(
        jnp.bfloat16
    )
    dest = lax.all_gather(mine, "mp", axis=0, tiled=True)
    whole_text = lax.all_gather(text[0], "mp", axis=2, tiled=True)
    seq_local = whole_text.shape[0]
    txt_len = whole_text.shape[1]
    tokens = seq_local * txt_len
    text_norm = (
        layer_norm(whole_text, text_gain[0])
        .astype(jnp.bfloat16)
        .reshape(tokens, whole_text.shape[2])
    )
    head_cols = w_query.shape[2]
    head_local = head_cols // HD
    query_sum = jnp.dot(
        text_norm,
        lax.all_gather(w_query[0], "dp", axis=0, tiled=True),
        preferred_element_type=jnp.float32,
    )
    query_matrix = query_sum.astype(jnp.bfloat16).reshape(seq_local, txt_len, head_local, HD)
    full_kv = lax.all_gather(w_kv[0], "dp", axis=0, tiled=True)
    pair_sum = jnp.einsum("lje,ekc->jlkc", dest, full_kv, preferred_element_type=jnp.float32)
    pair_list = pair_sum.astype(jnp.bfloat16).reshape(seq_local, FMAX * LAT, 2, head_local, HD)
    live = jnp.repeat(
        jnp.arange(FMAX, dtype=jnp.int32)[None, :] < frame_counts[0][:, None], LAT, axis=1
    )
    gate = jnp.tanh(xgate[0])

    def local_attend(pair_in):
        return jax.vmap(attend, in_axes=(0, 0, 0, None))(query_matrix, pair_in, live, gate)

    gated, pull = jax.vjp(local_attend, pair_list)
    context = gated.astype(jnp.bfloat16)[None]
    (pair_grad,) = pull(cotangent[0].astype(jnp.float32))
    pair_grad = pair_grad.reshape(owned, LAT, 2, head_cols)
    part = pair_grad
    dest_grad = lax.psum_scatter(
        jnp.einsum("jlkc,ekc->lje", part, full_kv, preferred_element_type=jnp.float32).astype(
            jnp.bfloat16
        ),
        "mp",
        scatter_dimension=0,
        tiled=True,
    ).astype(jnp.float32)
    every_grad = lax.all_gather(
        dest_grad.astype(jnp.bfloat16), ("segment", "dp"), axis=1, tiled=True
    ).astype(dest_grad.dtype)
    targets = lax.dynamic_slice_in_dim(frame_dest, group * owned, owned, 0)
    chooser = (jnp.arange(slots, dtype=jnp.int32)[None, :] == targets[:, None]).astype(jnp.float32)
    latent_grad = jnp.einsum("js,rse->rje", chooser, every_grad, precision=lax.Precision.HIGHEST)
    return (context, latent_grad)


def solution(mesh):
    in_specs = (
        P(("segment", "dp"), "mp", None),
        P(),
        P(),
        P(None, "mp"),
        P(None, None, "mp"),
        P(),
        P("segment", "dp", None, "mp"),
        P("segment", None),
        P("segment", "dp", "mp"),
        P("segment", "dp", None, "mp"),
        P("segment"),
        P("segment", "dp"),
        P(),
        P("segment", "dp", None, "mp"),
    )
    out_specs = (P("segment", "dp", None, "mp"), P("mp", ("segment", "dp"), None))
    return jax.shard_map(
        per_device, mesh=mesh, in_specs=in_specs, out_specs=out_specs, check_vma=False
    )
```

profile of v0, /device:TPU:1, one launch (start us, length us, event | category | flops | bytes accessed | tf_op | source)
XLA Modules:
  0.0 658.1 jit_solution(9813244482838572930)
XLA Ops:
  14.1 52.8 %all-gather.11.cloned.1.call-done = bf16[8,128,1536]{2,1,0:T(8,128)(2,1)} async-done(((bf16[8,8,1536]{2,1,0:T(8,128)(2,1)}), bf16[8,128,1536]{2,1,0:T(8,128)(2,1)}) %all-gather.11.cloned.1.call-update) | async-done | bytes 3145744 | tf_op jit(solution)/shard_map/all_gather | solution.py:91
  66.9 2.5 convert_reduce_fusion.1
  69.5 2.8 fusion.15
  79.0 75.6 %reduce-scatter.3.cloned.1.call-done = bf16[4,8,1536]{2,1,0:T(8,128)(2,1)} async-done(((bf16[64,8,1536]{2,1,0:T(8,128)(2,1)}), bf16[4,8,1536]{2,1,0:T(8,128)(2,1)}) %reduce-scatter.3.cloned.1.call-update) | async-done | bytes 98320 | tf_op jit(solution)/shard_map/reduce_scatter | solution.py:125
  158.4 2.1 copy.40
  160.6 38.4 %all-gather.13.cloned.1.call-done = bf16[4,128,1536]{2,0,1:T(4,128)(2,1)} async-done(((bf16[4,8,1536]{2,0,1:T(4,128)(2,1)}), bf16[4,128,1536]{2,0,1:T(4,128)(2,1)}) %all-gather.13.cloned.1.call-update) | async-done | bytes 1572880 | tf_op jit(solution)/shard_map/all_gather | solution.py:137
  199.0 2.4 fusion.49
  206.3 34.1 %all-gather.19.cloned.1.call-done = bf16[1,1536,2,512]{3,1,2,0:T(8,128)(2,1)} async-done(((bf16[1,384,2,512]{3,1,2,0:T(8,128)(2,1)}), bf16[1,1536,2,512]{3,1,2,0:T(8,128)(2,1)}) %all-gather.19.cloned.1.call-update) | async-done | bytes 3145744 | tf_op jit(solution)/shard_map/all_gather | solution.py:162
  240.4 50.8 %all-gather.15.cloned.1.call-done = bf16[64,8,1536]{2,1,0:T(8,128)(2,1)} async-done(((bf16[4,8,1536]{2,1,0:T(8,128)(2,1)}), bf16[64,8,1536]{2,1,0:T(8,128)(2,1)}) %all-gather.15.cloned.1.call-update) | async-done | bytes 1572880 | tf_op jit(solution)/shard_map/all_gather | solution.py:144
  291.2 4.1 fusion.69
  297.1 100.5 %all-gather.21.cloned.1.call-done = bf16[1,1,768,8192]{3,2,1,0:T(8,128)(2,1)} async-done(((bf16[1,1,768,512]{3,2,1,0:T(8,128)(2,1)}), bf16[1,1,768,8192]{3,2,1,0:T(8,128)(2,1)}) %all-gather.21.cloned.1.call-update) | async-done | bytes 12582928 | tf_op jit(solution)/shard_map/all_gather | solution.py:145
  397.7 6.4 convert_reduce_fusion
  404.0 8.0 %fusion.3 = f32[768]{0:T(1024)S(1)} fusion(bf16[1,1,768,8192]{3,2,1,0:T(8,128)(2,1)} %all-gather.21.cloned.1.call-done, f32[768]{0:T(1024)S(1)} %broadcast_multiply_fusion), kind=kLoop, calls=%fused_computation.5 | loop fusion | flops 25165056 | bytes 12589056 | tf_op jit(solution)/shard_map/reduce_sum | solution.py:17
  412.0 72.3 %all-gather.23.cloned.1.call-done = bf16[1,8192,512]{2,1,0:T(8,128)(2,1)} async-done(((bf16[1,2048,512]{2,1,0:T(8,128)(2,1)}), bf16[1,8192,512]{2,1,0:T(8,128)(2,1)}) %all-gather.23.cloned.1.call-update) | async-done | bytes 8388624 | tf_op jit(solution)/shard_map/all_gather | solution.py:158
  484.3 17.6 %fusion.64 = bf16[768,512]{0,1:T(8,128)(2,1)S(1)} fusion(bf16[1,8192,512]{2,1,0:T(8,128)(2,1)} %all-gather.23.cloned.1.call-done, bf16[1,1,768,8192]{3,2,1,0:T(8,128)(2,1)} %all-gather.21.cloned.1.call-done, f32[8192]{0:T(1024)S(1)} %bitcast.222, f32[768]{0:T(1024)S(1)} %add_rsqrt_fusion, f32[768]{0:T(1024)S(1)} %broadcast_multiply_fusion), kind=kOutput, calls=%fused_computation.65 | convolution fusion | flops 6474301440 | bytes 21796864 | tf_op jit(solution)/shard_map/dot_general | solution.py:156
  506.2 2.8 fusion.53
  508.9 7.0 %fusion.85 = bf16[1,512,1,4,128]{1,4,3,2,0:T(8,128)(2,1)} fusion(bf16[768,4,128]{0,2,1:T(8,128)(2,1)S(1)} %bitcast.217, f32[4,768,512]{1,2,0:T(8,128)} %copy-done.2, f32[4,768]{1,0:T(4,128)S(1)} %negate_bitcast_fusion, f32[4,768]{1,0:T(4,128)S(1)} %get-tuple-element.21, pred[512]{0:T(512)(128)(4,1)S(1)} %broadcast_in_dim.37, ...), kind=kOutput, calls=%fused_computation.70 | convolution fusion | flops 820117504 | bytes 9736704 | tf_op jit(solution)/shard_map/transpose(jvp(vmap(rag,lag->arl)))/dot_general | solution.py:22
  516.0 2.1 pad_add_fusion
  518.1 2.8 reshape.439
  520.9 3.4 copy.54
  524.2 5.3 fusion.44
  529.6 77.0 %reduce-scatter.5.cloned.1.call-done = bf16[4,8,1536]{2,1,0:T(8,128)(2,1)} async-done(((bf16[64,8,1536]{2,1,0:T(8,128)(2,1)}), bf16[4,8,1536]{2,1,0:T(8,128)(2,1)}) %reduce-scatter.5.cloned.1.call-update) | async-done | bytes 98320 | tf_op jit(solution)/shard_map/reduce_scatter | solution.py:178
  607.9 41.2 %all-gather.17.cloned.1.call-done = bf16[4,128,1536]{2,1,0:T(8,128)(2,1)} async-done(((bf16[4,8,1536]{2,1,0:T(8,128)(2,1)}), bf16[4,128,1536]{2,1,0:T(8,128)(2,1)}) %all-gather.17.cloned.1.call-update) | async-done | bytes 1572880 | tf_op jit(solution)/shard_map/all_gather | solution.py:186
  649.1 2.5 convolution_bitcast_fusion.1
  (82 shorter events, 28.2 us)
Async XLA Ops:
  7.2 3.9 copy-start
  7.2 59.8 %all-gather.11.cloned.1.call-start = ((), (), s32[]{:S(2)}) async-start(), calls=%async_computation.2 | async-start | bytes 3342336 | tf_op jit(solution)/shard_map/all_gather | solution.py:91
  7.9 146.7 %reduce-scatter.3.cloned.1.call-start = ((), (), s32[]{:S(2)}) async-start(), calls=%async_computation.3 | async-start | bytes 1671168 | tf_op jit(solution)/shard_map/reduce_scatter | solution.py:125
  66.9 5.4 copy-start.3
  73.8 125.2 %copy-start.8 = (s32[128]{0:T(128)S(1)}, s32[128]{0:T(128)}, u32[]{:S(2)}) copy-start(s32[128]{0:T(128)} %param.26) | copy-start | bytes 1540
  76.2 127.4 %copy-start.5 = (bf16[1,1,768,512]{3,2,1,0:T(8,128)(2,1)S(1)}, bf16[1,1,768,512]{3,2,1,0:T(8,128)(2,1)}, u32[]{:S(2)}) copy-start(bf16[1,1,768,512]{3,2,1,0:T(8,128)(2,1)} %param.27) | copy-start | bytes 2359300
  78.2 120.8 %all-gather.13.cloned.1.call-start = ((), (), s32[]{:S(2)}) async-start(), calls=%async_computation.4 | async-start | bytes 1671168 | tf_op jit(solution)/shard_map/all_gather | solution.py:137
  158.4 47.9 %copy-start.7 = (bf16[1,8192]{1,0:T(2,128)(2,1)S(1)}, bf16[1,8192]{1,0:T(2,128)(2,1)}, u32[]{:S(2)}) copy-start(bf16[1,8192]{1,0:T(2,128)(2,1)} %param.21) | copy-start | bytes 49156
  158.4 82.0 %all-gather.19.cloned.1.call-start = ((), (), s32[]{:S(2)}) async-start(), calls=%async_computation.8 | async-start | bytes 3932160 | tf_op jit(solution)/shard_map/all_gather | solution.py:162
  160.6 130.6 %all-gather.15.cloned.1.call-start = ((), (), s32[]{:S(2)}) async-start(), calls=%async_computation.5 | async-start | bytes 1671168 | tf_op jit(solution)/shard_map/all_gather | solution.py:144
  201.5 196.2 %all-gather.21.cloned.1.call-start = ((), (), s32[]{:S(2)}) async-start(), calls=%async_computation.9 | async-start | bytes 13369344 | tf_op jit(solution)/shard_map/all_gather | solution.py:145
  202.1 282.2 %all-gather.23.cloned.1.call-start = ((), (), s32[]{:S(2)}) async-start(), calls=%async_computation.10 | async-start | bytes 10485760 | tf_op jit(solution)/shard_map/all_gather | solution.py:158
  202.8 403.8 %reduce-scatter.5.cloned.1.call-start = ((), (), s32[]{:S(2)}) async-start(), calls=%async_computation.6 | async-start | bytes 1671168 | tf_op jit(solution)/shard_map/reduce_scatter | solution.py:178
  501.8 2.6 copy-start.4
  502.9 3.2 copy-start.2
  524.2 82.5 %copy-start.6 = (bf16[1,768,4,128]{1,3,2,0:T(8,128)(2,1)S(1)}, bf16[1,768,4,128]{1,3,2,0:T(8,128)(2,1)}, u32[]{:S(2)}) copy-start(bf16[1,768,4,128]{1,3,2,0:T(8,128)(2,1)} %get-tuple-element.14) | copy-start | bytes 2359300
  524.2 127.3 %copy-start.1 = (bf16[1536,2,96]{0,2,1:T(8,128)(2,1)S(1)}, bf16[1536,2,96]{0,2,1:T(8,128)(2,1)}, u32[]{:S(2)}) copy-start(bf16[1536,2,96]{0,2,1:T(8,128)(2,1)} %param.18) | copy-start | bytes 1769476
  529.6 119.5 %all-gather.17.cloned.1.call-start = ((), (), s32[]{:S(2)}) async-start(), calls=%async_computation.7 | async-start | bytes 1671168 | tf_op jit(solution)/shard_map/all_gather | solution.py:186
Sparse Core Ops, SparseCore 0:
  10.4 56.4 all-gather.10
  78.3 76.1 reduce-scatter.2
  158.5 40.4 all-gather.12
  201.3 39.1 all-gather.18
  243.3 47.8 all-gather.14
  293.5 104.1 all-gather.20
  399.5 84.7 all-gather.22
  529.7 76.8 reduce-scatter.4
  608.5 40.5 all-gather.16
where the time goes:
time: 659 us; the launch traced here: 658 us
  waiting for transfers between devices  545 us (83%)
  matrix products  50.9 us (8%)
  other arithmetic  30.7 us (5%)
  local copies, waits for them, and re-layouts  15.8 us (2%)
  between operations  15.5 us (2%)
    all_gather x1, waiting for transfers between devices, per_device(): whole_text = lax.all_gather(text[0], 'mp', axis=2, tiled=True)  101 us
    reduce_scatter x1, waiting for transfers between devices, per_device(): lax.psum_scatter(jnp.einsum('jlkc,ekc->lje', part, full_kv, preferred_ele...  77 us
    reduce_scatter x1, waiting for transfers between devices, per_device(): lax.psum_scatter(jnp.einsum('fhlr,hre->lfe', part, out_heads, preferred_e...  75.6 us
    all_gather x1, waiting for transfers between devices, per_device(): lax.all_gather(w_query[0], 'dp', axis=0, tiled=True)  72.3 us
    all_gather x1, waiting for transfers between devices, per_device(): piece = lax.all_gather(frames, 'mp', axis=1, tiled=True)  52.8 us
    all_gather x1, waiting for transfers between devices, per_device(): dest = lax.all_gather(mine, 'mp', axis=0, tiled=True)  50.8 us
    all_gather x1, waiting for transfers between devices, per_device(): lax.all_gather(dest_grad.astype(jnp.bfloat16), ('segment', 'dp'), axis=1,...  41.2 us
    all_gather x1, waiting for transfers between devices, per_device(): gathered = lax.all_gather(latents, ('segment', 'dp'), axis=1, tiled=True)  38.4 us
  transfers between devices with their start and end apart: 9, of which 9 were waited for; matrix products, arithmetic and copies ran while one was open for 5% of the time, Pallas kernels for 0%

commit v1 on v0

--- a/solution.py
+++ b/solution.py
@@ -88,7 +88,21 @@
         latent_pair_rows[:, 1],
         preferred_element_type=jnp.float32,
     )
-    piece = lax.all_gather(frames, "mp", axis=1, tiled=True)
+    ways, here, step = (lax.axis_size("mp"), lax.axis_index("mp"), frames.shape[1])
+    dims = [n * ways if d == 1 else n for d, n in enumerate(frames.shape)]
+    full = lax.dynamic_update_slice_in_dim(
+        jnp.zeros(dims, frames.dtype), frames, here * step, axis=1
+    )
+    going_up = going_down = frames
+    for far in range(1, ways // 2 + 1):
+        going_up = lax.ppermute(going_up, "mp", [(d, (d + 1) % ways) for d in range(ways)])
+        full = lax.dynamic_update_slice_in_dim(full, going_up, (here - far) % ways * step, axis=1)
+        if 2 * far < ways:
+            going_down = lax.ppermute(going_down, "mp", [(d, (d - 1) % ways) for d in range(ways)])
+            full = lax.dynamic_update_slice_in_dim(
+                full, going_down, (here + far) % ways * step, axis=1
+            )
+    piece = full
     run_max = jnp.broadcast_to(first_max, (owned,) + first_max.shape)
     run_sum = jnp.broadcast_to(first_sum, (owned,) + first_sum.shape)
     run_acc = jnp.broadcast_to(first_acc, (owned,) + first_acc.shape)

time: 659 us -> 688 us (1.044); the launches traced: 658 us -> 679 us
  starting transfers between devices: 0.36 us -> 37.9 us
  waiting for transfers between devices: 545 us -> 531 us
    all_gather x1 -> x0, waiting for transfers between devices: 52.8 us -> none  [per_device(): piece = lax.all_gather(frames, 'mp', axis=1, tiled=True)]
    ppermute x0 -> x15, starting transfers between devices: none -> 37.5 us  [the longest x7 37.1 us: per_device(): lax.ppermute(going_down, 'mp', [(d, (d - 1) % ways) for d in range(ways)])]
    ppermute x0 -> x15, waiting for transfers between devices: none -> 30.8 us  [the longest x8 17.6 us: per_device(): lax.ppermute(going_up, 'mp', [(d, (d + 1) % ways) for d in range(ways)])]
    reduce_scatter x1, waiting for transfers between devices: 75.6 us -> 82.9 us  [per_device(): lax.psum_scatter(jnp.einsum('fhlr,hre->lfe', part, out_heads, preferred_e...]
  transfers between devices with their start and end apart: 9 -> 23, of which waited for: 9 -> 15; matrix products, arithmetic and copies ran while one was open for 5% -> 5% of each run, Pallas kernels for 0% -> 0%
where the time goes in v1:
time: 688 us; the launch traced here: 679 us
  waiting for transfers between devices  531 us (77%)
  matrix products  50.9 us (7%)
  starting transfers between devices  37.9 us (6%)
  other arithmetic  26.8 us (4%)
  local copies, waits for them, and re-layouts  16.3 us (2%)
  between operations  16.2 us (2%)
    all_gather x1, waiting for transfers between devices, per_device(): whole_text = lax.all_gather(text[0], 'mp', axis=2, tiled=True)  101 us
    reduce_scatter x1, waiting for transfers between devices, per_device(): lax.psum_scatter(jnp.einsum('fhlr,hre->lfe', part, out_heads, preferred_e...  82.9 us
    reduce_scatter x1, waiting for transfers between devices, per_device(): lax.psum_scatter(jnp.einsum('jlkc,ekc->lje', part, full_kv, preferred_ele...  77 us
    all_gather x1, waiting for transfers between devices, per_device(): lax.all_gather(w_query[0], 'dp', axis=0, tiled=True)  72.1 us
    all_gather x1, waiting for transfers between devices, per_device(): dest = lax.all_gather(mine, 'mp', axis=0, tiled=True)  50.8 us
    all_gather x1, waiting for transfers between devices, per_device(): lax.all_gather(dest_grad.astype(jnp.bfloat16), ('segment', 'dp'), axis=1,...  41.2 us
    all_gather x1, waiting for transfers between devices, per_device(): gathered = lax.all_gather(latents, ('segment', 'dp'), axis=1, tiled=True)  39.6 us
    ppermute x7, starting transfers between devices, per_device(): lax.ppermute(going_down, 'mp', [(d, (d - 1) % ways) for d in range(ways)])  37.1 us
  transfers between devices with their start and end apart: 23, of which 15 were waited for; matrix products, arithmetic and copies ran while one was open for 5% of the time, Pallas kernels for 0%

profile of v1, /device:TPU:1, one launch (start us, length us, event | category | flops | bytes accessed | tf_op | source)
XLA Modules:
  0.0 678.7 jit_solution(10422884285585795815)
XLA Ops:
  7.2 5.8 collective-permute-start.1
  19.6 4.8 collective-permute-start.3
  27.4 5.5 collective-permute-start.5
  35.5 5.2 collective-permute-start.7
  43.4 5.2 collective-permute-start.9
  51.2 5.2 collective-permute-start.11
  59.0 5.2 collective-permute-start.13
  64.8 7.9 %collective-permute-done.12 = bf16[8,8,1536]{2,1,0:T(8,128)(2,1)S(1)} collective-permute-done((bf16[8,8,1536]{2,1,0:T(8,128)(2,1)S(1)}, bf16[8,8,1536]{2,1,0:T(8,128)(2,1)S(1)}, u32[]{:S(2)}, u32[]{:S(2)}) %collective-permute-start.12) | collective-permute-done | bytes 196640 | tf_op jit(solution)/shard_map/ppermute | solution.py:98
  72.8 9.7 %collective-permute-done.14 = bf16[8,8,1536]{2,1,0:T(8,128)(2,1)S(1)} collective-permute-done((bf16[8,8,1536]{2,1,0:T(8,128)(2,1)S(1)}, bf16[8,8,1536]{2,1,0:T(8,128)(2,1)S(1)}, u32[]{:S(2)}, u32[]{:S(2)}) %collective-permute-start.14) | collective-permute-done | bytes 196640 | tf_op jit(solution)/shard_map/ppermute | solution.py:98
  90.6 82.9 %reduce-scatter.3.cloned.1.call-done = bf16[4,8,1536]{2,1,0:T(8,128)(2,1)} async-done(((bf16[64,8,1536]{2,1,0:T(8,128)(2,1)}), bf16[4,8,1536]{2,1,0:T(8,128)(2,1)}) %reduce-scatter.3.cloned.1.call-update) | async-done | bytes 98320 | tf_op jit(solution)/shard_map/reduce_scatter | solution.py:139
  178.5 39.6 %all-gather.10.cloned.1.call-done = bf16[4,128,1536]{2,0,1:T(4,128)(2,1)} async-done(((bf16[4,8,1536]{2,0,1:T(4,128)(2,1)}), bf16[4,128,1536]{2,0,1:T(4,128)(2,1)}) %all-gather.10.cloned.1.call-update) | async-done | bytes 1572880 | tf_op jit(solution)/shard_map/all_gather | solution.py:151
  225.2 34.4 %all-gather.16.cloned.1.call-done = bf16[1,1536,2,512]{3,1,2,0:T(8,128)(2,1)} async-done(((bf16[1,384,2,512]{3,1,2,0:T(8,128)(2,1)}), bf16[1,1536,2,512]{3,1,2,0:T(8,128)(2,1)}) %all-gather.16.cloned.1.call-update) | async-done | bytes 3145744 | tf_op jit(solution)/shard_map/all_gather | solution.py:176
  259.6 50.8 %all-gather.12.cloned.1.call-done = bf16[64,8,1536]{2,1,0:T(8,128)(2,1)} async-done(((bf16[4,8,1536]{2,1,0:T(8,128)(2,1)}), bf16[64,8,1536]{2,1,0:T(8,128)(2,1)}) %all-gather.12.cloned.1.call-update) | async-done | bytes 1572880 | tf_op jit(solution)/shard_map/all_gather | solution.py:158
  310.4 4.1 fusion.69
  316.3 100.6 %all-gather.18.cloned.1.call-done = bf16[1,1,768,8192]{3,2,1,0:T(8,128)(2,1)} async-done(((bf16[1,1,768,512]{3,2,1,0:T(8,128)(2,1)}), bf16[1,1,768,8192]{3,2,1,0:T(8,128)(2,1)}) %all-gather.18.cloned.1.call-update) | async-done | bytes 12582928 | tf_op jit(solution)/shard_map/all_gather | solution.py:159
  416.8 6.4 convert_reduce_fusion
  423.2 8.0 %fusion.3 = f32[768]{0:T(1024)S(1)} fusion(bf16[1,1,768,8192]{3,2,1,0:T(8,128)(2,1)} %all-gather.18.cloned.1.call-done, f32[768]{0:T(1024)S(1)} %broadcast_multiply_fusion), kind=kLoop, calls=%fused_computation.5 | loop fusion | flops 25165056 | bytes 12589056 | tf_op jit(solution)/shard_map/reduce_sum | solution.py:17
  431.2 72.1 %all-gather.20.cloned.1.call-done = bf16[1,8192,512]{2,1,0:T(8,128)(2,1)} async-done(((bf16[1,2048,512]{2,1,0:T(8,128)(2,1)}), bf16[1,8192,512]{2,1,0:T(8,128)(2,1)}) %all-gather.20.cloned.1.call-update) | async-done | bytes 8388624 | tf_op jit(solution)/shard_map/all_gather | solution.py:172
  503.3 17.6 %fusion.64 = bf16[768,512]{0,1:T(8,128)(2,1)S(1)} fusion(bf16[1,8192,512]{2,1,0:T(8,128)(2,1)} %all-gather.20.cloned.1.call-done, bf16[1,1,768,8192]{3,2,1,0:T(8,128)(2,1)} %all-gather.18.cloned.1.call-done, f32[8192]{0:T(1024)S(1)} %bitcast.222, f32[768]{0:T(1024)S(1)} %add_rsqrt_fusion, f32[768]{0:T(1024)S(1)} %broadcast_multiply_fusion), kind=kOutput, calls=%fused_computation.65 | convolution fusion | flops 6474301440 | bytes 21796864 | tf_op jit(solution)/shard_map/dot_general | solution.py:170
  529.1 7.0 %fusion.85 = bf16[1,512,1,4,128]{1,4,3,2,0:T(8,128)(2,1)} fusion(bf16[768,4,128]{0,2,1:T(8,128)(2,1)S(1)} %bitcast.217, f32[4,768,512]{1,2,0:T(8,128)} %copy-done.2, f32[4,768]{1,0:T(4,128)S(1)} %negate_bitcast_fusion, f32[4,768]{1,0:T(4,128)S(1)} %get-tuple-element.21, pred[512]{0:T(512)(128)(4,1)S(1)} %broadcast_in_dim.40, ...), kind=kOutput, calls=%fused_computation.70 | convolution fusion | flops 820117504 | bytes 9736704 | tf_op jit(solution)/shard_map/transpose(jvp(vmap(rag,lag->arl)))/dot_general | solution.py:22
  541.0 3.4 copy.54
  544.4 5.3 fusion.44
  549.7 77.0 %reduce-scatter.5.cloned.1.call-done = bf16[4,8,1536]{2,1,0:T(8,128)(2,1)} async-done(((bf16[64,8,1536]{2,1,0:T(8,128)(2,1)}), bf16[4,8,1536]{2,1,0:T(8,128)(2,1)}) %reduce-scatter.5.cloned.1.call-update) | async-done | bytes 98320 | tf_op jit(solution)/shard_map/reduce_scatter | solution.py:192
  628.1 41.2 %all-gather.14.cloned.1.call-done = bf16[4,128,1536]{2,1,0:T(8,128)(2,1)} async-done(((bf16[4,8,1536]{2,1,0:T(8,128)(2,1)}), bf16[4,128,1536]{2,1,0:T(8,128)(2,1)}) %all-gather.14.cloned.1.call-update) | async-done | bytes 1572880 | tf_op jit(solution)/shard_map/all_gather | solution.py:200
  (128 shorter events, 57.5 us)
Async XLA Ops:
  7.2 166.4 %reduce-scatter.3.cloned.1.call-start = ((), (), s32[]{:S(2)}) async-start(), calls=%async_computation.2 | async-start | bytes 1671168 | tf_op jit(solution)/shard_map/reduce_scatter | solution.py:139
  7.2 12.4 %collective-permute-start.1 = (bf16[8,8,1536]{2,1,0:T(8,128)(2,1)}, bf16[8,8,1536]{2,1,0:T(8,128)(2,1)S(1)}, u32[]{:S(2)}, u32[]{:S(2)}) collective-permute-start(bf16[8,8,1536]{2,1,0:T(8,128)(2,1)} %param.14), channel_id=1, source_target_pairs={{0,60},{4,0},{8,4},{12,8},{16,12},{20,16},{24,20},{28,24},{32,28},... | collective-permute-start | bytes 589832 | tf_op jit(solution)/shard_map/ppermute | solution.py:101
  13.1 11.4 %collective-permute-start = (bf16[8,8,1536]{2,1,0:T(8,128)(2,1)}, bf16[8,8,1536]{2,1,0:T(8,128)(2,1)S(1)}, u32[]{:S(2)}, u32[]{:S(2)}) collective-permute-start(bf16[8,8,1536]{2,1,0:T(8,128)(2,1)} %param.14), channel_id=1, source_target_pairs={{0,4},{4,8},{8,12},{12,16},{16,20},{20,24},{24,28},{28,32},{32,36}... | collective-permute-start | bytes 589832 | tf_op jit(solution)/shard_map/ppermute | solution.py:98
  19.6 7.8 %collective-permute-start.3 = (bf16[8,8,1536]{2,1,0:T(8,128)(2,1)S(1)}, bf16[8,8,1536]{2,1,0:T(8,128)(2,1)S(1)}, u32[]{:S(2)}, u32[]{:S(2)}) collective-permute-start(bf16[8,8,1536]{2,1,0:T(8,128)(2,1)S(1)} %collective-permute-done.1), channel_id=1, source_target_pairs={{0,60},{4,0},{8,4},{12,8},{16,12},{20,16},{24,20},{28,24},{32,28},... | collective-permute-start | bytes 589832 | tf_op jit(solution)/shard_map/ppermute | solution.py:101
  24.4 8.5 %collective-permute-start.2 = (bf16[8,8,1536]{2,1,0:T(8,128)(2,1)S(1)}, bf16[8,8,1536]{2,1,0:T(8,128)(2,1)S(1)}, u32[]{:S(2)}, u32[]{:S(2)}) collective-permute-start(bf16[8,8,1536]{2,1,0:T(8,128)(2,1)S(1)} %collective-permute-done), channel_id=1, source_target_pairs={{0,4},{4,8},{8,12},{12,16},{16,20},{20,24},{24,28},{28,32},{32,36}... | collective-permute-start | bytes 589832 | tf_op jit(solution)/shard_map/ppermute | solution.py:98
  27.4 8.1 %collective-permute-start.5 = (bf16[8,8,1536]{2,1,0:T(8,128)(2,1)S(1)}, bf16[8,8,1536]{2,1,0:T(8,128)(2,1)S(1)}, u32[]{:S(2)}, u32[]{:S(2)}) collective-permute-start(bf16[8,8,1536]{2,1,0:T(8,128)(2,1)S(1)} %collective-permute-done.3), channel_id=1, source_target_pairs={{0,60},{4,0},{8,4},{12,8},{16,12},{20,16},{24,20},{28,24},{32,28},... | collective-permute-start | bytes 589832 | tf_op jit(solution)/shard_map/ppermute | solution.py:101
  32.9 7.8 %collective-permute-start.4 = (bf16[8,8,1536]{2,1,0:T(8,128)(2,1)S(1)}, bf16[8,8,1536]{2,1,0:T(8,128)(2,1)S(1)}, u32[]{:S(2)}, u32[]{:S(2)}) collective-permute-start(bf16[8,8,1536]{2,1,0:T(8,128)(2,1)S(1)} %collective-permute-done.2), channel_id=1, source_target_pairs={{0,4},{4,8},{8,12},{12,16},{16,20},{20,24},{24,28},{28,32},{32,36}... | collective-permute-start | bytes 589832 | tf_op jit(solution)/shard_map/ppermute | solution.py:98
  35.5 7.8 %collective-permute-start.7 = (bf16[8,8,1536]{2,1,0:T(8,128)(2,1)S(1)}, bf16[8,8,1536]{2,1,0:T(8,128)(2,1)S(1)}, u32[]{:S(2)}, u32[]{:S(2)}) collective-permute-start(bf16[8,8,1536]{2,1,0:T(8,128)(2,1)S(1)} %collective-permute-done.5), channel_id=1, source_target_pairs={{0,60},{4,0},{8,4},{12,8},{16,12},{20,16},{24,20},{28,24},{32,28},... | collective-permute-start | bytes 589832 | tf_op jit(solution)/shard_map/ppermute | solution.py:101
  40.7 7.8 %collective-permute-start.6 = (bf16[8,8,1536]{2,1,0:T(8,128)(2,1)S(1)}, bf16[8,8,1536]{2,1,0:T(8,128)(2,1)S(1)}, u32[]{:S(2)}, u32[]{:S(2)}) collective-permute-start(bf16[8,8,1536]{2,1,0:T(8,128)(2,1)S(1)} %collective-permute-done.4), channel_id=1, source_target_pairs={{0,4},{4,8},{8,12},{12,16},{16,20},{20,24},{24,28},{28,32},{32,36}... | collective-permute-start | bytes 589832 | tf_op jit(solution)/shard_map/ppermute | solution.py:98
  43.4 7.8 %collective-permute-start.9 = (bf16[8,8,1536]{2,1,0:T(8,128)(2,1)S(1)}, bf16[8,8,1536]{2,1,0:T(8,128)(2,1)S(1)}, u32[]{:S(2)}, u32[]{:S(2)}) collective-permute-start(bf16[8,8,1536]{2,1,0:T(8,128)(2,1)S(1)} %collective-permute-done.7), channel_id=1, source_target_pairs={{0,60},{4,0},{8,4},{12,8},{16,12},{20,16},{24,20},{28,24},{32,28},... | collective-permute-start | bytes 589832 | tf_op jit(solution)/shard_map/ppermute | solution.py:101
  48.6 7.8 %collective-permute-start.8 = (bf16[8,8,1536]{2,1,0:T(8,128)(2,1)S(1)}, bf16[8,8,1536]{2,1,0:T(8,128)(2,1)S(1)}, u32[]{:S(2)}, u32[]{:S(2)}) collective-permute-start(bf16[8,8,1536]{2,1,0:T(8,128)(2,1)S(1)} %collective-permute-done.6), channel_id=1, source_target_pairs={{0,4},{4,8},{8,12},{12,16},{16,20},{20,24},{24,28},{28,32},{32,36}... | collective-permute-start | bytes 589832 | tf_op jit(solution)/shard_map/ppermute | solution.py:98
  51.2 7.8 %collective-permute-start.11 = (bf16[8,8,1536]{2,1,0:T(8,128)(2,1)S(1)}, bf16[8,8,1536]{2,1,0:T(8,128)(2,1)S(1)}, u32[]{:S(2)}, u32[]{:S(2)}) collective-permute-start(bf16[8,8,1536]{2,1,0:T(8,128)(2,1)S(1)} %collective-permute-done.9), channel_id=1, source_target_pairs={{0,60},{4,0},{8,4},{12,8},{16,12},{20,16},{24,20},{28,24},{32,28},... | collective-permute-start | bytes 589832 | tf_op jit(solution)/shard_map/ppermute | solution.py:101
  56.4 7.8 %collective-permute-start.10 = (bf16[8,8,1536]{2,1,0:T(8,128)(2,1)S(1)}, bf16[8,8,1536]{2,1,0:T(8,128)(2,1)S(1)}, u32[]{:S(2)}, u32[]{:S(2)}) collective-permute-start(bf16[8,8,1536]{2,1,0:T(8,128)(2,1)S(1)} %collective-permute-done.8), channel_id=1, source_target_pairs={{0,4},{4,8},{8,12},{12,16},{16,20},{20,24},{24,28},{28,32},{32,36}... | collective-permute-start | bytes 589832 | tf_op jit(solution)/shard_map/ppermute | solution.py:98
  59.0 13.7 %collective-permute-start.13 = (bf16[8,8,1536]{2,1,0:T(8,128)(2,1)S(1)}, bf16[8,8,1536]{2,1,0:T(8,128)(2,1)S(1)}, u32[]{:S(2)}, u32[]{:S(2)}) collective-permute-start(bf16[8,8,1536]{2,1,0:T(8,128)(2,1)S(1)} %collective-permute-done.11), channel_id=1, source_target_pairs={{0,60},{4,0},{8,4},{12,8},{16,12},{20,16},{24,20},{28,24},{32,28},... | collective-permute-start | bytes 589832 | tf_op jit(solution)/shard_map/ppermute | solution.py:101
  64.3 8.5 %collective-permute-start.12 = (bf16[8,8,1536]{2,1,0:T(8,128)(2,1)S(1)}, bf16[8,8,1536]{2,1,0:T(8,128)(2,1)S(1)}, u32[]{:S(2)}, u32[]{:S(2)}) collective-permute-start(bf16[8,8,1536]{2,1,0:T(8,128)(2,1)S(1)} %collective-permute-done.10), channel_id=1, source_target_pairs={{0,4},{4,8},{8,12},{12,16},{16,20},{20,24},{24,28},{28,32},{32,36}... | collective-permute-start | bytes 589832 | tf_op jit(solution)/shard_map/ppermute | solution.py:98
  72.7 9.8 %collective-permute-start.14 = (bf16[8,8,1536]{2,1,0:T(8,128)(2,1)S(1)}, bf16[8,8,1536]{2,1,0:T(8,128)(2,1)S(1)}, u32[]{:S(2)}, u32[]{:S(2)}) collective-permute-start(bf16[8,8,1536]{2,1,0:T(8,128)(2,1)S(1)} %collective-permute-done.12), channel_id=1, source_target_pairs={{0,4},{4,8},{8,12},{12,16},{16,20},{20,24},{24,28},{28,32},{32,36}... | collective-permute-start | bytes 589832 | tf_op jit(solution)/shard_map/ppermute | solution.py:98
  89.8 128.3 %copy-start.9 = (s32[128]{0:T(128)S(1)}, s32[128]{0:T(128)}, u32[]{:S(2)}) copy-start(s32[128]{0:T(128)} %param.26) | copy-start | bytes 1540
  89.8 128.2 %all-gather.10.cloned.1.call-start = ((), (), s32[]{:S(2)}) async-start(), calls=%async_computation.3 | async-start | bytes 1671168 | tf_op jit(solution)/shard_map/all_gather | solution.py:151
  177.4 82.3 %all-gather.16.cloned.1.call-start = ((), (), s32[]{:S(2)}) async-start(), calls=%async_computation.7 | async-start | bytes 3932160 | tf_op jit(solution)/shard_map/all_gather | solution.py:176
  178.4 132.0 %all-gather.12.cloned.1.call-start = ((), (), s32[]{:S(2)}) async-start(), calls=%async_computation.4 | async-start | bytes 1671168 | tf_op jit(solution)/shard_map/all_gather | solution.py:158
  220.5 196.3 %all-gather.18.cloned.1.call-start = ((), (), s32[]{:S(2)}) async-start(), calls=%async_computation.8 | async-start | bytes 13369344 | tf_op jit(solution)/shard_map/all_gather | solution.py:159
  221.1 282.2 %all-gather.20.cloned.1.call-start = ((), (), s32[]{:S(2)}) async-start(), calls=%async_computation.9 | async-start | bytes 10485760 | tf_op jit(solution)/shard_map/all_gather | solution.py:172
  221.7 405.1 %reduce-scatter.5.cloned.1.call-start = ((), (), s32[]{:S(2)}) async-start(), calls=%async_computation.5 | async-start | bytes 1671168 | tf_op jit(solution)/shard_map/reduce_scatter | solution.py:192
  549.7 119.5 %all-gather.14.cloned.1.call-start = ((), (), s32[]{:S(2)}) async-start(), calls=%async_computation.6 | async-start | bytes 1671168 | tf_op jit(solution)/shard_map/all_gather | solution.py:200
  (9 other events, 418.7 us)
Sparse Core Ops, SparseCore 0:
  90.0 83.5 reduce-scatter.2
  177.5 40.5 all-gather.9
  220.5 39.1 all-gather.15
  262.5 47.8 all-gather.11
  312.6 104.1 all-gather.17
  418.5 84.7 all-gather.19
  549.8 76.9 reduce-scatter.4
  628.6 40.5 all-gather.13
